TPU v7x, 512 devices: a whole 4x4x16 slice. The times are simulated.
512 devices in a mesh: gx: 16 (over x, y_hi, core), gy: 32 (over y_lo, z).
Axes of the slice: x: 4, y: 4 (y_hi: 2, y_lo: 2; y = y_hi * 2 + y_lo), z: 16, core: 2. Of those that a mesh axis runs over, the one named last changes fastest.
Arguments:
- query: bfloat16 [128, 3584], P('gy', 'gx'), may hold values from -48 to 48
- prefix_keys: bfloat16 [262144, 512], P(('gx', 'gy')), may hold values from -16 to 16
- prefix_values: bfloat16 [262144, 512], P(('gx', 'gy')), may hold values from -6 to 6
- suffix_keys: bfloat16 [128, 256, 512], P('gy', 'gx'), may hold values from -9 to 9
- suffix_values: bfloat16 [128, 256, 512], P('gy', 'gx'), may hold values from -6 to 6
- suffix_lengths: int32 [128], P('gy'), may hold values from 1 to 256, as said below
- out_weight: bfloat16 [3584, 3584], P('gx'), may hold values from -0.09375 to 0.09375
Outputs:
- attended: bfloat16 [128, 3584], P('gy', 'gx')
Inputs may be any that keep to these rules, and one draw needn't show every extreme that they name: `suffix_lengths`: some sample has exactly 256 live slots.
All inputs are finite; a program needn't handle non-finite values.
Results may differ from a plain program's by a relative error of at most 0.0051.
Values may be sent and summed in bfloat16 or wider, within the bound.
A program may use at most 64 MiB of HBM per device.

v0:
```python
import math

import jax
import jax.numpy as jnp
from jax import lax
from jax.sharding import PartitionSpec as P

HQ = 28
KVH = 4
HD = 128


def on_device(
    query, prefix_keys, prefix_values, suffix_keys, suffix_values, suffix_lengths, out_weight
):
    group = HQ // KVH
    scale = 1.0 / math.sqrt(HD)
    widened = lax.all_gather(query, "gx", axis=1, tiled=True)
    full_query = lax.all_gather(widened, "gy", axis=0, tiled=True)
    samples = full_query.shape[0]
    owned = query.shape[0]
    slots = suffix_keys.shape[1]
    row_start = lax.axis_index("gy") * owned
    dims = (((1,), (1,)), ((), ()))

    def group_scores(g):
        block_query = full_query[:, g * group * HD : (g + 1) * group * HD].reshape(
            samples * group, HD
        )
        keys = prefix_keys[:, g * HD : (g + 1) * HD]
        return lax.dot_general(block_query, keys, dims, preferred_element_type=jnp.float32) * scale

    maxima = jnp.concatenate(
        [jnp.max(group_scores(g), axis=1).reshape(samples, group) for g in range(KVH)], axis=1
    )
    own_query = lax.dynamic_slice_in_dim(full_query, row_start, owned, 0).reshape(
        owned, KVH, group, HD
    )
    own_keys = suffix_keys.reshape(owned, slots, KVH, HD)
    own_values = suffix_values.reshape(owned, slots, KVH, HD)
    suffix_scores = (
        jnp.einsum("sghd,stgd->sght", own_query, own_keys, preferred_element_type=jnp.float32)
        * scale
    )
    positions = lax.axis_index("gx") * slots + jnp.arange(slots, dtype=jnp.int32)
    valid = (positions[None, :] < suffix_lengths[:, None])[:, None, None, :]
    masked = jnp.where(valid, suffix_scores, jnp.float32(-1e30))
    suffix_max = jnp.max(masked, axis=-1).reshape(owned, HQ)
    own_max = jnp.maximum(lax.dynamic_slice_in_dim(maxima, row_start, owned, 0), suffix_max)
    local_max = lax.dynamic_update_slice_in_dim(maxima, own_max, row_start, 0)
    top = lax.pmax(local_max, ("gx", "gy"))
    numer_parts = []
    denom_parts = []
    for g in range(KVH):
        top_group = top[:, g * group : (g + 1) * group].reshape(samples * group)
        probs = jnp.exp(group_scores(g) - top_group[:, None])
        denom_parts.append(jnp.sum(probs, axis=1).reshape(samples, group))
        weighted = jnp.dot(
            probs.astype(jnp.bfloat16),
            prefix_values[:, g * HD : (g + 1) * HD],
            preferred_element_type=jnp.float32,
        )
        numer_parts.append(weighted.reshape(samples, group * HD))
    numer = jnp.concatenate(numer_parts, axis=1)
    denom = jnp.concatenate(denom_parts, axis=1)
    own_top = lax.dynamic_slice_in_dim(top, row_start, owned, 0).reshape(owned, KVH, group)
    suffix_probs = jnp.where(valid, jnp.exp(masked - own_top[..., None]), jnp.float32(0.0))
    suffix_total = jnp.sum(suffix_probs, axis=-1).reshape(owned, HQ)
    suffix_out = jnp.einsum(
        "sght,stgd->sghd",
        suffix_probs.astype(jnp.bfloat16),
        own_values,
        preferred_element_type=jnp.float32,
    ).reshape(owned, HQ * HD)
    numer = lax.dynamic_update_slice_in_dim(
        numer, lax.dynamic_slice_in_dim(numer, row_start, owned, 0) + suffix_out, row_start, 0
    )
    denom = lax.dynamic_update_slice_in_dim(
        denom, lax.dynamic_slice_in_dim(denom, row_start, owned, 0) + suffix_total, row_start, 0
    )
    total_numer, total_denom = lax.psum((numer, denom), ("gx", "gy"))
    owned_numer = lax.dynamic_slice_in_dim(total_numer, row_start, owned, 0)
    owned_denom = lax.dynamic_slice_in_dim(total_denom, row_start, owned, 0)
    heads = (
        (owned_numer.reshape(owned, HQ, HD) / owned_denom[:, :, None])
        .astype(jnp.bfloat16)
        .reshape(owned, HQ * HD)
    )
    feature_count = out_weight.shape[0]
    feature_start = lax.axis_index("gx") * feature_count
    own_heads = lax.dynamic_slice_in_dim(heads, feature_start, feature_count, 1)
    partial_out = jnp.dot(own_heads, out_weight, preferred_element_type=jnp.float32)
    return lax.psum_scatter(partial_out, "gx", scatter_dimension=1, tiled=True).astype(jnp.bfloat16)


def solution(mesh):
    return jax.shard_map(
        on_device,
        mesh=mesh,
        in_specs=(
            P("gy", "gx"),
            P(("gx", "gy"), None),
            P(("gx", "gy"), None),
            P("gy", "gx", None),
            P("gy", "gx", None),
            P("gy"),
            P("gx", None),
        ),
        out_specs=P("gy", "gx"),
        check_vma=False,
    )
```

profile of v0, /device:TPU:1, one launch (start us, length us, event | category | flops | bytes accessed | tf_op | source)
XLA Modules:
  0.0 824.8 jit_solution(12647078765586853012)
XLA Ops:
  6.5 26.2 %all-gather = bf16[16,224,4]{1,2,0:T(4,128)(2,1)S(1)} all-gather(bf16[1,224,4]{1,2,0:T(4,128)(2,1)} %bitcast.41), channel_id=1, replica_groups=mesh['gx'=16,'gy'=32] {'gx'}, dimensions={0}, use_global_device_ids=true | all-gather | bytes 30464 | tf_op jit(solution)/shard_map/all_gather | solution.py:18
  32.8 60.1 %all-gather.1 = bf16[32,4,3584]{2,1,0:T(4,128)(2,1)S(1)} all-gather(bf16[1,4,3584]{2,1,0:T(4,128)(2,1)S(1)} %bitcast.39), channel_id=1, replica_groups=mesh['gx'=16,'gy'=32] {'gy'}, dimensions={0}, use_global_device_ids=true | all-gather | bytes 946176 | tf_op jit(solution)/shard_map/all_gather | solution.py:19
  99.6 2.7 multiply_reduce_fusion.1
  103.0 2.6 multiply_reduce_fusion
  106.5 2.7 multiply_reduce_fusion.3
  110.0 1.7 pad_maximum_fusion
  112.9 110.7 %pmax.7 = f32[128,28]{1,0:T(8,128)S(1)} all-reduce(f32[128,28]{1,0:T(8,128)} %constant_dynamic-update-slice_fusion.5), channel_id=1, replica_groups=mesh['gx'=16,'gy'=32] {'gx','gy'}, use_global_device_ids=true, to_apply=%region_5.6 | all-reduce | flops 3584 | bytes 28672 | tf_op jit(solution)/shard_map/pmax | solution.py:51
  224.5 1.7 fusion.37
  231.3 2.2 fusion.13
  233.4 1.9 reshape.118
  235.3 2.8 fusion.11
  238.1 1.9 reshape.119
  240.0 2.8 fusion.9
  242.7 1.9 reshape.120
  244.6 2.7 fusion.15
  247.4 1.9 reshape.117
  249.3 1.9 constant_dynamic-update-slice_fusion.3
  251.2 1.9 constant_dynamic-update-slice_fusion.2
  256.4 2.0 fusion.4
  263.1 100.8 %psum.15 = f32[128,28]{1,0:T(8,128)S(1)} all-reduce(f32[128,28]{1,0:T(8,128)S(1)} %constant_dynamic-update-slice_fusion.4), channel_id=1, replica_groups=mesh['gx'=16,'gy'=32] {'gx','gy'}, use_global_device_ids=true, to_apply=%region_12.13 | all-reduce | flops 3584 | bytes 28672 | tf_op jit(solution)/shard_map/psum | solution.py:81
  364.0 357.7 %all-reduce.2.cloned.1.call-done = f32[128,3584]{1,0:T(8,128)} async-done(((f32[128,3584]{1,0:T(8,128)}), f32[128,3584]{1,0:T(8,128)}) %all-reduce.2.cloned.1.call-update) | async-done | bytes 1835024 | tf_op jit(solution)/shard_map/psum | solution.py:81
  721.7 2.9 convolution_bitcast_fusion
  724.6 91.8 %reduce-scatter.4.cloned.1.call-done = f32[224,4]{1,0:T(8,128)} async-done(((f32[3584,4]{1,0:T(8,128)}), f32[224,4]{1,0:T(8,128)}) %reduce-scatter.4.cloned.1.call-update) | async-done | bytes 3600
  816.4 1.6 copy.38
  (65 shorter events, 24.5 us)
Async XLA Ops:
  6.5 715.2 %copy-start = (bf16[224,3584]{1,0:T(8,128)(2,1)S(1)}, bf16[224,3584]{1,0:T(8,128)(2,1)}, u32[]{:S(2)}) copy-start(bf16[224,3584]{1,0:T(8,128)(2,1)} %param.13) | copy-start | bytes 4816900
  6.5 715.2 %all-reduce.2.cloned.1.call-start = ((), (), s32[]{:S(2)}) async-start(), calls=%async_computation.1 | async-start | bytes 3670016 | tf_op jit(solution)/shard_map/psum | solution.py:81
  92.9 1.3 copy-start.7
  92.9 1.4 copy-start.6
  249.3 3.8 copy-start.3
  249.3 4.7 copy-start.4
  256.3 560.1 %reduce-scatter.4.cloned.1.call-start = ((), (), s32[]{:S(2)}) async-start(), calls=%async_computation.2 | async-start | bytes 1949696
  256.4 2.1 copy-start.1
  256.4 2.6 copy-start.2
  258.4 1.0 copy-start.5
Sparse Core Ops, SparseCore 0:
  256.5 465.2 all-reduce.1
  726.5 89.8 reduce-scatter.3
where the time goes:
time: 827 us; the launch traced here: 825 us
  waiting for transfers between devices  450 us (54%)
  blocking collectives  298 us (36%)
  local copies, waits for them, and re-layouts  30.1 us (4%)
  matrix products  25.2 us (3%)
  between operations  13.5 us (2%)
  other arithmetic  8.71 us (1%)
    psum x1, waiting for transfers between devices, on_device(): total_numer, total_denom = lax.psum((numer, denom), ('gx', 'gy'))  358 us
    pmax x1, blocking collectives, on_device(): top = lax.pmax(local_max, ('gx', 'gy'))  111 us
    psum x1, blocking collectives, on_device(): total_numer, total_denom = lax.psum((numer, denom), ('gx', 'gy'))  101 us
    unnamed x3, waiting for transfers between devices  91.8 us
    all_gather x1, blocking collectives, on_device(): full_query = lax.all_gather(widened, 'gy', axis=0, tiled=True)  60.1 us
    all_gather x1, blocking collectives, on_device(): widened = lax.all_gather(query, 'gx', axis=1, tiled=True)  26.2 us
  transfers between devices with their start and end apart: 2, of which 2 were waited for; matrix products, arithmetic and copies ran while one was open for 1% of the time, Pallas kernels for 0%

commit v1 on v0

v1 whole, which is shorter than its diff:
```python
import math

import jax
import jax.numpy as jnp
from jax import lax
from jax.experimental import pallas as pl
from jax.experimental.pallas import tpu as pltpu
from jax.sharding import PartitionSpec as P

MESH = pl.DeviceIdType.MESH
F32, BF16 = jnp.float32, jnp.bfloat16
HD = 128
SCALE = math.log2(math.e) / math.sqrt(HD)
ROW_DIMS = (((1,), (1,)), ((), ()))


def iota(shape, axis):
    return lax.broadcasted_iota(jnp.int32, shape, axis)


def with_stats(values, top, total, split):
    lane, row = iota((1, 8, 128), 2), iota((1, 8, 128), 1)
    if split:
        high = total.astype(BF16).astype(F32)
        low = jnp.where(lane == row + 16, total - high, 0.0)
        total = high
    else:
        low = 0.0
    stats = jnp.where(lane == row, total, 0.0) + jnp.where(lane == row + 8, top, 0.0) + low
    return jnp.where(row == 7, jnp.sum(stats, axis=1, keepdims=True), values)


def read_stats(tiles, split):
    lane, row = iota((1, 8, 128), 2), iota((1, 8, 128), 1)
    last = tiles[:, 7:8, :]
    here = lane == row
    if split:
        here = here | (lane == row + 16)
    total = jnp.sum(jnp.where(here, last, 0.0), axis=2, keepdims=True)
    top = jnp.sum(jnp.where(lane == row + 8, last, 0.0), axis=2, keepdims=True)
    return top, total


def merge(parts):
    top = parts[0][1]
    for part in parts[1:]:
        top = jnp.maximum(top, part[1])
    values, total = 0.0, 0.0
    for part_values, part_top, part_total in parts:
        weight = jnp.exp2(part_top - top)
        values = values + weight * part_values
        total = total + weight * part_total
    return values, top, total


def kernel(
    q_ref, k_hbm, v_hbm, sk_hbm, sv_hbm, len_ref, w_hbm, o_ref,
    kbuf, vbuf, wraw, wp, sbuf, sfx, ztile, qsend, qall, xf, qf, s_ref,
    osend, orecv, zsend, zrecv, hbuf, psend, precv,
    local_sem, k_ss, k_rs, v_ss, v_rs, s_ss, s_rs, r_ss, r_rs, l_ss, l_rs,
    qa_ss, qa_rs, o_ss, o_rs, z_ss, z_rs, h_ss, h_rs, p_ss, p_rs,
):
    gx, gy = lax.axis_index("gx"), lax.axis_index("gy")
    x, yh, c = gx // 4, (gx // 2) % 2, gx % 2
    yl, z = gy // 16, gy % 16
    y = 2 * yh + yl

    def dev(x_=None, y_=None, c_=None, z_=None):
        x_ = x if x_ is None else x_
        y_ = y if y_ is None else y_
        c_ = c if c_ is None else c_
        z_ = z if z_ is None else z_
        return (x_ * 4 + (y_ // 2) * 2 + c_, (y_ % 2) * 16 + z_)

    def lanes(i):
        return pl.ds(pl.multiple_of(i * HD, HD), HD)

    sent = []

    def send(src, dst, ss, rs, to):
        copy = pltpu.make_async_remote_copy(
            src_ref=src, dst_ref=dst, send_sem=ss, recv_sem=rs, device_id=to, device_id_type=MESH
        )
        copy.start()
        sent.append(copy)

    def arrived(dst, rs):
        pltpu.make_async_remote_copy(
            src_ref=dst, dst_ref=dst, send_sem=rs, recv_sem=rs, device_id=dev(z_=(z + 1) % 16),
            device_id_type=MESH,
        ).wait_recv()

    around = [dev(z_=(z + 1) % 16), dev(z_=(z + 15) % 16)]
    around += [dev(x_=(x + d) % 4) for d in (1, 2, 3)]
    partners = [(dy, dc) for dy in (2, 1, 3, 0) for dc in (0, 1) if dy or dc]
    around += [dev(y_=(y + dy) % 4, c_=(c + dc) % 2) for dy, dc in partners]
    barrier = pltpu.get_barrier_semaphore()
    for to in around:
        pl.semaphore_signal(barrier, inc=1, device_id=to, device_id_type=MESH)

    local = [
        pltpu.make_async_copy(k_hbm.at[:, lanes(x)], kbuf.at[0], local_sem.at[0]),
        pltpu.make_async_copy(v_hbm.at[:, lanes(x)], vbuf.at[0], local_sem.at[1]),
        pltpu.make_async_copy(w_hbm, wraw, local_sem.at[2]),
    ]
    for g in range(4):
        for at, ref in enumerate((sk_hbm, sv_hbm)):
            local.append(
                pltpu.make_async_copy(
                    ref.at[:, :, g * HD : (g + 1) * HD], sbuf.at[g, :, at], local_sem.at[3 + 2 * g + at]
                )
            )
    for copy in local:
        copy.start()
    query = q_ref[...].astype(F32)
    ztile[8] = jnp.zeros((8, 128), F32)
    ztile[8, pl.ds(0, 4, stride=2), :] = query[:, 0:128]
    ztile[8, pl.ds(1, 4, stride=2), 0:96] = query[:, 128:224]

    pl.semaphore_wait(barrier, len(around))

    for d in (2, 1, 3):
        to = (x + d) % 4
        send(k_hbm.at[:, lanes(to)], kbuf.at[d], k_ss.at[d], k_rs.at[d], dev(x_=to))
    for d in (2, 1, 3):
        to = (x + d) % 4
        send(v_hbm.at[:, lanes(to)], vbuf.at[d], v_ss.at[d], v_rs.at[d], dev(x_=to))

    mine = yl * 4 + 2 * yh + c

    def to_partners(piece, first, count):
        rows = pl.ds(first * 8, count * 8)
        packed = ztile[first : first + count].reshape(count * 8, 128).astype(BF16)
        qall[mine, rows, :] = packed
        qsend[rows, :] = packed
        for at, (dy, dc) in enumerate(partners):
            send(
                qsend.at[rows], qall.at[mine, rows], qa_ss.at[piece, at], qa_rs.at[piece, mine],
                dev(y_=(y + dy) % 4, c_=(c + dc) % 2),
            )

    for s in range(8):
        if s:
            arrived(ztile.at[8 - s], r_rs.at[8 - s])
        send(ztile.at[8 - s], ztile.at[7 - s], r_ss.at[s], r_rs.at[7 - s], dev(z_=(z + 1) % 16))
        if s:
            arrived(ztile.at[8 + s], l_rs.at[8 + s])
        if s < 7:
            send(ztile.at[8 + s], ztile.at[9 + s], l_ss.at[s], l_rs.at[9 + s], dev(z_=(z + 15) % 16))
        if s == 4:
            to_partners(0, 4, 8)
    to_partners(1, 12, 4)
    arrived(ztile.at[0], r_rs.at[0])
    to_partners(2, 0, 4)

    local[2].wait()
    wp[:, 224:256, :] = jnp.zeros((16, 32, 256), BF16)
    lane = iota((224, 128), 1)

    def relay(q, carry):
        for r in range(4):
            first, off = (224 * r) // 128, (224 * r) % 128
            tiles = []
            for n in range(3):
                if n < 2 or off >= 64:
                    at = pl.multiple_of(q * 896 + (first + n) * 128, 128)
                    tile = wraw[:, pl.ds(at, 128)].astype(F32)
                    tiles.append(pltpu.roll(tile, 128 - off, 1) if off else tile)
                else:
                    tiles.append(jnp.zeros((224, 128), F32))
            for n in range(2):
                block = jnp.where(lane < 128 - off, tiles[n], tiles[n + 1])
                wp[q * 4 + r, 0:224, n * 128 : (n + 1) * 128] = block.astype(BF16)
        return carry

    lax.fori_loop(0, 4, relay, 0)

    for dy, dc in partners:
        source = (y + dy) % 4
        source = (source % 2) * 4 + (source // 2) * 2 + (c + dc) % 2
        for piece, (first, count) in enumerate(((4, 8), (12, 4), (0, 4))):
            arrived(qall.at[source, pl.ds(first * 8, count * 8)], qa_rs.at[piece, source])
    lane = iota((16, 128), 1)
    xf[...] = qall[...].astype(F32)
    qf[...] = jnp.zeros_like(qf)
    for at in range(8):
        t = at % 4
        pieces = []
        for b in range(4):
            for half in range(2):
                pieces.append(xf[at // 4 * 4 + b, pl.ds(2 * t + half, 16, stride=8), :])
        starts = [224 * (n // 2) + 128 * (n % 2) for n in range(8)]
        sizes = [128 if n % 2 == 0 else 96 for n in range(8)]
        for h in range(7):
            head = None
            for n in range(8):
                low = max(starts[n], 128 * h)
                high = min(starts[n] + sizes[n], 128 * h + 128)
                if low < high:
                    shift = (starts[n] - 128 * h) % 128
                    moved = pltpu.roll(pieces[n], shift, 1) if shift else pieces[n]
                    if head is None:
                        head = moved
                    else:
                        head = jnp.where(lane < low - 128 * h, head, moved)
            qf[at, pl.ds(h, 16, stride=8), :] = head

    local[0].wait()
    local[1].wait()
    for copy in local[3:]:
        copy.wait()
    for d in (2, 1, 3):
        arrived(kbuf.at[d], k_rs.at[d])
    for d in (2, 1, 3):
        arrived(vbuf.at[d], v_rs.at[d])

    sfx[gx] = sbuf[x, 2 * yh + c]
    for d in range(1, 16):
        to = (gx + d) % 16
        send(sbuf.at[to // 4, to % 4], sfx.at[gx], s_ss.at[d], s_rs.at[gx], (to, gy))

    for dy in (2, 1, 3, 0):
        to_y = (y + dy) % 4
        first = (to_y % 2) * 4 + (to_y // 2) * 2
        rows = qf[pl.ds(first, 2)].reshape(256, 128).astype(BF16)
        top = None
        for n in range(4):
            scores = lax.dot_general(rows, kbuf[n], ROW_DIMS, preferred_element_type=F32)
            s_ref[:, n * 512 : (n + 1) * 512] = scores
            for m in range(4):
                part = scores[:, m * 128 : (m + 1) * 128]
                top = part if top is None else jnp.maximum(top, part)
        top = (jnp.max(top, axis=1, keepdims=True) * SCALE).astype(BF16).astype(F32)
        total, values = 0.0, 0.0
        for n in range(4):
            probs = jnp.exp2(s_ref[:, n * 512 : (n + 1) * 512] * SCALE - top)
            for m in range(4):
                total = total + probs[:, m * 128 : (m + 1) * 128]
            values = values + jnp.dot(probs.astype(BF16), vbuf[n], preferred_element_type=F32)
        total = jnp.sum(total, axis=1, keepdims=True)
        packed = with_stats(
            values.reshape(32, 8, 128), top.reshape(32, 8, 1), total.reshape(32, 8, 1), True
        )
        osend[dy] = packed.reshape(2, 128, 128).astype(BF16)
        if dy:
            for to_c in range(2):
                send(
                    osend.at[dy, to_c], orecv.at[dy * 2 + c], o_ss.at[dy * 2 + to_c], o_rs.at[dy * 2 + c],
                    dev(y_=to_y, c_=to_c),
                )
        else:
            send(osend.at[0, 1 - c], orecv.at[c], o_ss.at[0], o_rs.at[c], dev(c_=1 - c))
            orecv[c] = osend[0, c]

    for d in range(1, 16):
        source = (gx + d) % 16
        arrived(sfx.at[source], s_rs.at[source])
    own = qf[mine, 64:72, :].astype(BF16)
    suffix_keys = sfx[:, 0].reshape(256, 128)
    suffix_values = sfx[:, 1].reshape(256, 128)
    scores = lax.dot_general(own, suffix_keys, ROW_DIMS, preferred_element_type=F32) * SCALE
    live = iota((8, 256), 1) < len_ref[2 * yh + c]
    scores = jnp.where(live, scores, -1e30)
    suffix_top = jnp.max(scores, axis=1, keepdims=True)
    probs = jnp.where(live, jnp.exp2(scores - suffix_top), 0.0)
    suffix_total = jnp.sum(probs, axis=1, keepdims=True)
    suffix_out = jnp.dot(probs.astype(BF16), suffix_values, preferred_element_type=F32)

    for dy in (2, 1, 3):
        for from_c in range(2):
            arrived(orecv.at[dy * 2 + from_c], o_rs.at[dy * 2 + from_c])
    arrived(orecv.at[1 - c], o_rs.at[1 - c])
    parts = []
    for n in range(8):
        tiles = orecv[n].astype(F32).reshape(16, 8, 128)
        parts.append((tiles,) + read_stats(tiles, True))
    zsend[...] = with_stats(*merge(parts), False)

    for p in (0, 1, 15, 2, 14, 3, 13, 4, 12, 5, 11, 6, 10, 7, 9):
        send(zsend.at[p], zrecv.at[p], z_ss.at[p], z_rs.at[p], dev(z_=(z + p + 8) % 16))
    zrecv[8] = zsend[8]
    for p in range(16):
        if p != 8:
            arrived(zrecv.at[p], z_rs.at[p])
    tiles = zrecv[...]
    tops, totals = read_stats(tiles, False)
    parts = [(tiles[p], tops[p], totals[p]) for p in range(16)]
    parts.append((suffix_out, suffix_top, suffix_total))
    values, _, total = merge(parts)
    heads = jnp.where(iota((8, 128), 0) < 7, values / total, 0.0)

    hbuf[2 * yh + c] = heads
    for at, (dyh, dc) in enumerate(((1, 0), (1, 1), (0, 1))):
        to = dev(y_=(y + 2 * dyh) % 4, c_=(c + dc) % 2)
        send(hbuf.at[2 * yh + c], hbuf.at[2 * yh + c], h_ss.at[at], h_rs.at[2 * yh + c], to)
    for dyh, dc in ((1, 0), (1, 1), (0, 1)):
        source = 2 * ((yh + dyh) % 2) + (c + dc) % 2
        arrived(hbuf.at[source], h_rs.at[source])

    feature = 224 * (2 * yh + c)
    head, off = feature // 128, feature % 128
    lane = iota((8, 128), 1)
    moved = []
    for n in range(3):
        four = jnp.concatenate([hbuf[t, pl.ds(head + n, 1), :] for t in range(4)], axis=0)
        eight = jnp.concatenate([four, four], axis=0)
        moved.append(pltpu.roll(eight, (128 - off) % 128, 1))
    left = jnp.where(lane < 128 - off, moved[0], moved[1])
    right = jnp.where(lane < 128 - off, moved[1], moved[2])
    right = jnp.where(lane < 96, right, 0.0)
    features = jnp.concatenate([left, right], axis=1).astype(BF16)
    row = iota((8, 128), 0)
    for d in tuple(range(1, 16)) + (0,):
        to = (gx + d) % 16
        product = jnp.dot(features, wp[to], preferred_element_type=F32)
        tile = jnp.where(row < 4, product[:, 0:128], product[:, 128:256])
        if d:
            psend[d] = tile
            send(psend.at[d], precv.at[d], p_ss.at[d], p_rs.at[d], (to, gy))
        else:
            result = tile
    for d in range(1, 16):
        arrived(precv.at[d], p_rs.at[d])
    for d in range(1, 16):
        result = result + precv[d]
    o_ref[:, 0:128] = result[0:4].astype(BF16)
    o_ref[:, 128:224] = result[4:8, 0:96].astype(BF16)
    for copy in sent:
        copy.wait_send()


def on_device(query, keys, values, suffix_keys, suffix_values, lengths, out_weight):
    vmem = pl.BlockSpec(memory_space=pltpu.VMEM)
    hbm = pl.BlockSpec(memory_space=pl.ANY)
    dma = pltpu.SemaphoreType.DMA
    return pl.pallas_call(
        kernel,
        out_shape=jax.ShapeDtypeStruct((4, 224), BF16),
        in_specs=[vmem, hbm, hbm, hbm, hbm, pl.BlockSpec(memory_space=pltpu.SMEM), hbm],
        out_specs=vmem,
        scratch_shapes=[
            pltpu.VMEM((4, 512, 128), BF16),
            pltpu.VMEM((4, 512, 128), BF16),
            pltpu.VMEM((224, 3584), BF16),
            pltpu.VMEM((16, 256, 256), BF16),
            pltpu.VMEM((4, 4, 2, 16, 128), BF16),
            pltpu.VMEM((16, 2, 16, 128), BF16),
            pltpu.VMEM((16, 8, 128), F32),
            pltpu.VMEM((128, 128), BF16),
            pltpu.VMEM((8, 128, 128), BF16),
            pltpu.VMEM((8, 128, 128), F32),
            pltpu.VMEM((8, 128, 128), F32),
            pltpu.VMEM((256, 2048), F32),
            pltpu.VMEM((4, 2, 128, 128), BF16),
            pltpu.VMEM((8, 128, 128), BF16),
            pltpu.VMEM((16, 8, 128), F32),
            pltpu.VMEM((16, 8, 128), F32),
            pltpu.VMEM((4, 8, 128), F32),
            pltpu.VMEM((16, 8, 128), F32),
            pltpu.VMEM((16, 8, 128), F32),
            dma((11,)),
            dma((4,)), dma((4,)), dma((4,)), dma((4,)),
            dma((16,)), dma((16,)),
            dma((8,)), dma((8,)), dma((8,)), dma((16,)),
            dma((3, 7)), dma((3, 8)),
            dma((8,)), dma((8,)),
            dma((16,)), dma((16,)),
            dma((3,)), dma((4,)),
            dma((16,)), dma((16,)),
        ],
        compiler_params=pltpu.CompilerParams(
            collective_id=0, has_side_effects=True, vmem_limit_bytes=40 * 2**20
        ),
        name="decode_attention",
    )(query, keys, values, suffix_keys, suffix_values, lengths, out_weight)


def solution(mesh):
    return jax.shard_map(
        on_device,
        mesh=mesh,
        in_specs=(
            P("gy", "gx"),
            P(("gx", "gy"), None),
            P(("gx", "gy"), None),
            P("gy", "gx", None),
            P("gy", "gx", None),
            P("gy"),
            P("gx", None),
        ),
        out_specs=P("gy", "gx"),
        check_vma=False,
    )
```

time: 827 us -> 73 us (0.09)
  waiting for transfers between devices: 450 us -> 0 us
  blocking collectives: 298 us -> 0 us
  Pallas kernels: 0 us -> 65.5 us
  matrix products: 25.2 us -> 0 us
  local copies, waits for them, and re-layouts: 30.1 us -> 7.09 us
  between operations: 13.5 us -> 0.02 us
  other arithmetic: 8.71 us -> 0 us
    psum x1 -> x0, waiting for transfers between devices: 358 us -> none  [on_device(): total_numer, total_denom = lax.psum((numer, denom), ('gx', 'gy'))]
    pmax x1 -> x0, blocking collectives: 111 us -> none  [on_device(): top = lax.pmax(local_max, ('gx', 'gy'))]
    psum x1 -> x0, blocking collectives: 101 us -> none  [on_device(): total_numer, total_denom = lax.psum((numer, denom), ('gx', 'gy'))]
    unnamed x3 -> x0, waiting for transfers between devices: 91.8 us -> none
    all_gather x2 -> x0, blocking collectives: 86.2 us -> none  [the longest x1 60.1 us: on_device(): full_query = lax.all_gather(widened, 'gy', axis=0, tiled=True)]
    pallas_call x0 -> x1, Pallas kernels: none -> 65.5 us  [on_device(): pl.pallas_call(kernel, out_shape=jax.ShapeDtypeStruct((4, 224), BF16), in...]
    dot_general x10 -> x0, matrix products: 22.3 us -> none  [the longest x4 10.4 us: on_device(): jnp.dot(probs.astype(jnp.bfloat16), prefix_values[:, g * HD:(g + 1) * HD]...]
    reshape x20 -> x0, local copies, waits for them, and re-layouts: 17.1 us -> none  [the longest x4 7.58 us: on_device(): numer_parts.append(weighted.reshape(samples, group * HD))]
  transfers between devices with their start and end apart: 2 -> 0, of which waited for: 2 -> 0; matrix products, arithmetic and copies ran while one was open for 1% -> 0% of each run, Pallas kernels for 0% -> 0%
where the time goes in v1:
time: 73 us; the launch traced here: 72.7 us
  Pallas kernels  65.5 us (90%)
  local copies, waits for them, and re-layouts  7.09 us (10%)
    pallas_call x1, Pallas kernels, on_device(): pl.pallas_call(kernel, out_shape=jax.ShapeDtypeStruct((4, 224), BF16), in...  65.5 us
    unnamed x15, local copies, waits for them, and re-layouts  7.09 us

profile of v1, /device:TPU:1, one launch (start us, length us, event | category | flops | bytes accessed | tf_op | source)
XLA Modules:
  0.0 72.7 jit_solution(13875756521193032349)
XLA Ops:
  0.0 0.0 copy-start
  0.0 1.4 %copy-done = bf16[224,3584]{1,0:T(8,128)(2,1)S(1)} copy-done((bf16[224,3584]{1,0:T(8,128)(2,1)S(1)}, bf16[224,3584]{1,0:T(8,128)(2,1)}, u32[]{:S(2)}) %copy-start) | copy-done | bytes 1605656
  1.4 0.0 copy-start.1
  1.4 1.0 %copy-done.1 = bf16[512,512]{1,0:T(8,128)(2,1)S(1)} copy-done((bf16[512,512]{1,0:T(8,128)(2,1)S(1)}, bf16[512,512]{1,0:T(8,128)(2,1)}, u32[]{:S(2)}) %copy-start.1) | copy-done | bytes 524312
  2.5 0.0 copy-start.2
  2.5 1.0 %copy-done.2 = bf16[512,512]{1,0:T(8,128)(2,1)S(1)} copy-done((bf16[512,512]{1,0:T(8,128)(2,1)S(1)}, bf16[512,512]{1,0:T(8,128)(2,1)}, u32[]{:S(2)}) %copy-start.2) | copy-done | bytes 524312
  3.5 0.0 copy-start.3
  3.5 0.8 %copy-done.3 = bf16[4,16,512]{2,1,0:T(8,128)(2,1)S(1)} copy-done((bf16[4,16,512]{2,1,0:T(8,128)(2,1)S(1)}, bf16[4,16,512]{2,1,0:T(8,128)(2,1)}, u32[]{:S(2)}) %copy-start.3) | copy-done | bytes 65560
  4.3 0.0 copy-start.4
  4.3 0.8 %copy-done.4 = bf16[4,16,512]{2,1,0:T(8,128)(2,1)S(1)} copy-done((bf16[4,16,512]{2,1,0:T(8,128)(2,1)S(1)}, bf16[4,16,512]{2,1,0:T(8,128)(2,1)}, u32[]{:S(2)}) %copy-start.4) | copy-done | bytes 65560
  5.2 0.0 copy-start.5
  5.2 0.7 copy-done.5
  5.9 0.0 copy-start.6
  5.9 0.7 copy-done.6
  6.5 65.5 %decode_attention.1 = bf16[4,224]{1,0:T(4,128)(2,1)S(1)} custom-call(bf16[4,224]{1,0:T(4,128)(2,1)S(1)} %copy-done.5, bf16[512,512]{1,0:T(8,128)(2,1)S(1)} %copy-done.1, bf16[512,512]{1,0:T(8,128)(2,1)S(1)} %copy-done.2, bf16[4,16,512]{2,1,0:T(8,128)(2,1)S(1)} %copy-done.3, bf16[4,16,512]{2,1,0:T(8,128)(2,1)S(1)} %copy-done.4, s32[4]{0:T(128)S(1)} %copy-done.6, ...), custom_call_target="tpu_custom_call" | custom-call | tf_op jit(solution)/shard_map/decode_attention/pallas_call | solution.py:336
  72.1 0.6 copy.9
Async XLA Ops:
  0.0 1.4 %copy-start = (bf16[224,3584]{1,0:T(8,128)(2,1)S(1)}, bf16[224,3584]{1,0:T(8,128)(2,1)}, u32[]{:S(2)}) copy-start(bf16[224,3584]{1,0:T(8,128)(2,1)} %w_hbm.1) | copy-start | bytes 4816900
  1.4 1.0 %copy-start.1 = (bf16[512,512]{1,0:T(8,128)(2,1)S(1)}, bf16[512,512]{1,0:T(8,128)(2,1)}, u32[]{:S(2)}) copy-start(bf16[512,512]{1,0:T(8,128)(2,1)} %k_hbm.1) | copy-start | bytes 1572868
  2.5 1.0 %copy-start.2 = (bf16[512,512]{1,0:T(8,128)(2,1)S(1)}, bf16[512,512]{1,0:T(8,128)(2,1)}, u32[]{:S(2)}) copy-start(bf16[512,512]{1,0:T(8,128)(2,1)} %v_hbm.1) | copy-start | bytes 1572868
  3.5 0.8 %copy-start.3 = (bf16[4,16,512]{2,1,0:T(8,128)(2,1)S(1)}, bf16[4,16,512]{2,1,0:T(8,128)(2,1)}, u32[]{:S(2)}) copy-start(bf16[4,16,512]{2,1,0:T(8,128)(2,1)} %sk_hbm.1) | copy-start | bytes 196612
  4.3 0.8 %copy-start.4 = (bf16[4,16,512]{2,1,0:T(8,128)(2,1)S(1)}, bf16[4,16,512]{2,1,0:T(8,128)(2,1)}, u32[]{:S(2)}) copy-start(bf16[4,16,512]{2,1,0:T(8,128)(2,1)} %sv_hbm.1) | copy-start | bytes 196612
  5.2 0.7 copy-start.5
  5.9 0.7 copy-start.6

commit v2 on v1

--- a/solution.py
+++ b/solution.py
@@ -54,10 +54,10 @@
 
 
 def kernel(
-    q_ref, k_hbm, v_hbm, sk_hbm, sv_hbm, len_ref, w_hbm, o_ref,
-    kbuf, vbuf, wraw, wp, sbuf, sfx, ztile, qsend, qall, xf, qf, s_ref,
+    q_hbm, k_hbm, v_hbm, sk_hbm, sv_hbm, len_hbm, w_hbm, o_ref,
+    q_ref, len_ref, kbuf, vbuf, wraw, wp, sbuf, sfx, ztile, qsend, qall, xf, qf, s_ref,
     osend, orecv, zsend, zrecv, hbuf, psend, precv,
-    local_sem, k_ss, k_rs, v_ss, v_rs, s_ss, s_rs, r_ss, r_rs, l_ss, l_rs,
+    local_sem, k_ss, k_rs, v_ss, v_rs, s_ss, s_rs, r_ss, r_rs,
     qa_ss, qa_rs, o_ss, o_rs, z_ss, z_rs, h_ss, h_rs, p_ss, p_rs,
 ):
     gx, gy = lax.axis_index("gx"), lax.axis_index("gy")
@@ -90,7 +90,7 @@
             device_id_type=MESH,
         ).wait_recv()
 
-    around = [dev(z_=(z + 1) % 16), dev(z_=(z + 15) % 16)]
+    around = [dev(z_=(z + hops) % 16) for hops in (1, 2, 3, 4, 12, 13, 14, 15)]
     around += [dev(x_=(x + d) % 4) for d in (1, 2, 3)]
     partners = [(dy, dc) for dy in (2, 1, 3, 0) for dc in (0, 1) if dy or dc]
     around += [dev(y_=(y + dy) % 4, c_=(c + dc) % 2) for dy, dc in partners]
@@ -110,8 +110,12 @@
                     ref.at[:, :, g * HD : (g + 1) * HD], sbuf.at[g, :, at], local_sem.at[3 + 2 * g + at]
                 )
             )
+    local.append(pltpu.make_async_copy(len_hbm, len_ref, local_sem.at[11]))
+    fetch = pltpu.make_async_copy(q_hbm, q_ref, local_sem.at[12])
+    fetch.start()
     for copy in local:
         copy.start()
+    fetch.wait()
     query = q_ref[...].astype(F32)
     ztile[8] = jnp.zeros((8, 128), F32)
     ztile[8, pl.ds(0, 4, stride=2), :] = query[:, 0:128]
@@ -139,18 +143,29 @@
                 dev(y_=(y + dy) % 4, c_=(c + dc) % 2),
             )
 
-    for s in range(8):
-        if s:
-            arrived(ztile.at[8 - s], r_rs.at[8 - s])
-        send(ztile.at[8 - s], ztile.at[7 - s], r_ss.at[s], r_rs.at[7 - s], dev(z_=(z + 1) % 16))
-        if s:
-            arrived(ztile.at[8 + s], l_rs.at[8 + s])
-        if s < 7:
-            send(ztile.at[8 + s], ztile.at[9 + s], l_ss.at[s], l_rs.at[9 + s], dev(z_=(z + 15) % 16))
-        if s == 4:
-            to_partners(0, 4, 8)
+    def along_z(first, count, to_first, slot, hops):
+        send(
+            ztile.at[pl.ds(first, count)], ztile.at[pl.ds(to_first, count)], r_ss.at[slot], r_rs.at[slot],
+            dev(z_=(z + 16 + hops) % 16),
+        )
+
+    def from_z(first, count, slot):
+        arrived(ztile.at[pl.ds(first, count)], r_rs.at[slot])
+
+    for hops in (4, 3, 2, 1):
+        along_z(8, 1, 8 - hops, 8 - hops, hops)
+        along_z(8, 1, 8 + hops, 8 + hops, -hops)
+    for p in (7, 6, 5, 4):
+        from_z(p, 1, p)
+    along_z(4, 4, 0, 0, 4)
+    for p in (9, 10, 11):
+        from_z(p, 1, p)
+    along_z(9, 3, 13, 13, -4)
+    to_partners(0, 4, 8)
+    from_z(12, 1, 12)
+    from_z(13, 3, 13)
     to_partners(1, 12, 4)
-    arrived(ztile.at[0], r_rs.at[0])
+    from_z(0, 4, 0)
     to_partners(2, 0, 4)
 
     local[2].wait()
@@ -330,15 +345,16 @@
 
 
 def on_device(query, keys, values, suffix_keys, suffix_values, lengths, out_weight):
-    vmem = pl.BlockSpec(memory_space=pltpu.VMEM)
-    hbm = pl.BlockSpec(memory_space=pl.ANY)
+    hbm = pl.BlockSpec(memory_space=pltpu.HBM)
     dma = pltpu.SemaphoreType.DMA
     return pl.pallas_call(
         kernel,
         out_shape=jax.ShapeDtypeStruct((4, 224), BF16),
-        in_specs=[vmem, hbm, hbm, hbm, hbm, pl.BlockSpec(memory_space=pltpu.SMEM), hbm],
-        out_specs=vmem,
+        in_specs=[hbm] * 7,
+        out_specs=pl.BlockSpec(memory_space=pltpu.VMEM),
         scratch_shapes=[
+            pltpu.VMEM((4, 224), BF16),
+            pltpu.SMEM((4,), jnp.int32),
             pltpu.VMEM((4, 512, 128), BF16),
             pltpu.VMEM((4, 512, 128), BF16),
             pltpu.VMEM((224, 3584), BF16),
@@ -358,10 +374,10 @@
             pltpu.VMEM((4, 8, 128), F32),
             pltpu.VMEM((16, 8, 128), F32),
             pltpu.VMEM((16, 8, 128), F32),
-            dma((11,)),
+            dma((13,)),
             dma((4,)), dma((4,)), dma((4,)), dma((4,)),
             dma((16,)), dma((16,)),
-            dma((8,)), dma((8,)), dma((8,)), dma((16,)),
+            dma((16,)), dma((16,)),
             dma((3, 7)), dma((3, 8)),
             dma((8,)), dma((8,)),
             dma((16,)), dma((16,)),
@@ -369,7 +385,7 @@
             dma((16,)), dma((16,)),
         ],
         compiler_params=pltpu.CompilerParams(
-            collective_id=0, has_side_effects=True, vmem_limit_bytes=40 * 2**20
+            collective_id=0, has_side_effects=True, vmem_limit_bytes=56 * 2**20
         ),
         name="decode_attention",
     )(query, keys, values, suffix_keys, suffix_values, lengths, out_weight)

time: 73 us -> 56.1 us (0.77)
  Pallas kernels: 65.5 us -> 54.6 us
  local copies, waits for them, and re-layouts: 7.09 us -> 1.26 us
    pallas_call x1, Pallas kernels: 65.5 us -> 54.6 us  [on_device(): pl.pallas_call(kernel, out_shape=jax.ShapeDtypeStruct((4, 224), BF16), in...]
    unnamed x15 -> x1, local copies, waits for them, and re-layouts: 7.09 us -> 1.26 us
where the time goes in v2:
time: 56.1 us; the launch traced here: 55.9 us
  Pallas kernels  54.6 us (97%)
  local copies, waits for them, and re-layouts  1.26 us (2%)
    pallas_call x1, Pallas kernels, on_device(): pl.pallas_call(kernel, out_shape=jax.ShapeDtypeStruct((4, 224), BF16), in...  54.6 us
    unnamed x1, local copies, waits for them, and re-layouts  1.26 us

profile of v2, /device:TPU:1, one launch (start us, length us, event | category | flops | bytes accessed | tf_op | source)
XLA Modules:
  0.0 55.9 jit_solution(17722435572449390780)
XLA Ops:
  0.0 54.6 %decode_attention.1 = bf16[4,224]{1,0:T(4,128)(2,1)} custom-call(bf16[4,224]{1,0:T(4,128)(2,1)} %q_hbm.1, bf16[512,512]{1,0:T(8,128)(2,1)} %k_hbm.1, bf16[512,512]{1,0:T(8,128)(2,1)} %v_hbm.1, bf16[4,16,512]{2,1,0:T(8,128)(2,1)} %sk_hbm.1, bf16[4,16,512]{2,1,0:T(8,128)(2,1)} %sv_hbm.1, s32[4]{0:T(128)} %len_hbm.1, bf16[224,3584]{1,0:T(8,128)(2,1)} %w_hbm.1), custom_call_target="tpu_custom_call" | custom-call | tf_op jit(solution)/shard_map/decode_attention/pallas_call | solution.py:350
  54.6 1.3 %copy.9 = bf16[4,224]{1,0:T(4,128)(2,1)} copy(bf16[4,224]{1,0:T(4,128)(2,1)} %decode_attention.1) | data formatting | bytes 3584

commit v3 on v2

v3 whole, which is shorter than its diff:
```python
import math

import jax
import jax.numpy as jnp
from jax import lax
from jax.experimental import pallas as pl
from jax.experimental.pallas import tpu as pltpu
from jax.sharding import PartitionSpec as P

MESH = pl.DeviceIdType.MESH
F32, BF16 = jnp.float32, jnp.bfloat16
HD = 128
SCALE = math.log2(math.e) / math.sqrt(HD)
ROW_DIMS = (((1,), (1,)), ((), ()))


def iota(shape, axis):
    return lax.broadcasted_iota(jnp.int32, shape, axis)


def spread(weights, selector):
    high = weights.astype(BF16).astype(F32)
    both = high + pltpu.roll(weights - high, 16, 1)
    wide = jnp.dot(both.astype(BF16), selector, preferred_element_type=F32)
    return wide[:, 0:128], wide[:, 128:256]


def stats(tops, totals, split):
    lane = iota((1, 128), 1)
    out = 0.0
    for i in range(3):
        out = out + jnp.where(lane == 96 + i, tops[i], 0.0)
        if split:
            high = totals[i].astype(BF16).astype(F32)
            out = out + jnp.where(lane == 100 + i, high, 0.0) + jnp.where(lane == 104 + i, totals[i] - high, 0.0)
        else:
            out = out + jnp.where(lane == 100 + i, totals[i], 0.0)
    return out


def kernel(
    q_hbm, k_hbm, v_hbm, sk_hbm, sv_hbm, len_hbm, w_hbm, o_ref,
    q_ref, len_ref, kbuf, vbuf, wraw, wp, sbuf, sfx, ztile, qsend, qall, xf, qf, s_ref,
    acc, tops, totals, selector, osend, orecv, zsend, zrecv, ssend, srecv, psend, precv,
    local_sem, k_ss, k_rs, v_ss, v_rs, s_ss, s_rs, r_ss, r_rs, f_ss,
    qa_ss, qa_rs, o_ss, o_rs, z_ss, z_rs, h_ss, h_rs, p_ss, p_rs,
):
    gx, gy = lax.axis_index("gx"), lax.axis_index("gy")
    x, yh, c = gx // 4, (gx // 2) % 2, gx % 2
    yl, z = gy // 16, gy % 16
    y = 2 * yh + yl

    def dev(x_=None, y_=None, c_=None, z_=None):
        x_ = x if x_ is None else x_
        y_ = y if y_ is None else y_
        c_ = c if c_ is None else c_
        z_ = z if z_ is None else z_
        return (x_ * 4 + (y_ // 2) * 2 + c_, (y_ % 2) * 16 + z_)

    def lanes(i):
        return pl.ds(pl.multiple_of(i * HD, HD), HD)

    sent = []

    def send(src, dst, ss, rs, to):
        copy = pltpu.make_async_remote_copy(
            src_ref=src, dst_ref=dst, send_sem=ss, recv_sem=rs, device_id=to, device_id_type=MESH
        )
        copy.start()
        sent.append(copy)

    def arrived(dst, rs):
        pltpu.make_async_remote_copy(
            src_ref=dst, dst_ref=dst, send_sem=rs, recv_sem=rs, device_id=dev(z_=(z + 1) % 16),
            device_id_type=MESH,
        ).wait_recv()

    around = [dev(z_=(z + hops) % 16) for hops in (1, 2, 3, 4, 12, 13, 14, 15)]
    around += [dev(x_=(x + d) % 4) for d in (1, 2, 3)]
    partners = [(dy, dc) for dy in (2, 1, 3, 0) for dc in (0, 1) if dy or dc]
    around += [dev(y_=(y + dy) % 4, c_=(c + dc) % 2) for dy, dc in partners]
    barrier = pltpu.get_barrier_semaphore()
    for to in around:
        pl.semaphore_signal(barrier, inc=1, device_id=to, device_id_type=MESH)

    local = [
        pltpu.make_async_copy(k_hbm.at[:, lanes(x)], kbuf.at[0], local_sem.at[0]),
        pltpu.make_async_copy(v_hbm.at[:, lanes(x)], vbuf.at[0], local_sem.at[1]),
        pltpu.make_async_copy(w_hbm, wraw, local_sem.at[2]),
    ]
    for g in range(4):
        for at, ref in enumerate((sk_hbm, sv_hbm)):
            local.append(
                pltpu.make_async_copy(
                    ref.at[:, :, g * HD : (g + 1) * HD], sbuf.at[g, :, at], local_sem.at[3 + 2 * g + at]
                )
            )
    local.append(pltpu.make_async_copy(len_hbm, len_ref, local_sem.at[11]))
    fetch = pltpu.make_async_copy(q_hbm, q_ref, local_sem.at[12])
    fetch.start()
    pl.semaphore_wait(barrier, len(around))

    for group in ((1, 3), (2,)):
        for d in group:
            to = (x + d) % 4
            send(k_hbm.at[:, lanes(to)], kbuf.at[d], k_ss.at[d], k_rs.at[d], dev(x_=to))
        for d in group:
            to = (x + d) % 4
            send(v_hbm.at[:, lanes(to)], vbuf.at[d], v_ss.at[d], v_rs.at[d], dev(x_=to))

    fetch.wait()
    query = q_ref[...].astype(F32)
    ztile[8] = jnp.zeros((8, 128), F32)
    ztile[8, pl.ds(0, 4, stride=2), :] = query[:, 0:128]
    ztile[8, pl.ds(1, 4, stride=2), 0:96] = query[:, 128:224]
    for hops in (4, 3, 2, 1):
        for way in (hops, -hops):
            to = dev(z_=(z + 16 + way) % 16)
            send(ztile.at[8], ztile.at[8 - way], r_ss.at[8 - way], r_rs.at[8 - way], to)
    for copy in local:
        copy.start()

    local[2].wait()
    wp[:, 224:256, :] = jnp.zeros((16, 32, 256), BF16)
    lane = iota((224, 128), 1)

    def relay(q, carry):
        for r in range(4):
            first, off = (224 * r) // 128, (224 * r) % 128
            tiles = []
            for n in range(3):
                if n < 2 or off >= 64:
                    at = pl.multiple_of(q * 896 + (first + n) * 128, 128)
                    tile = wraw[:, pl.ds(at, 128)].astype(F32)
                    tiles.append(pltpu.roll(tile, 128 - off, 1) if off else tile)
                else:
                    tiles.append(jnp.zeros((224, 128), F32))
            for n in range(2):
                block = jnp.where(lane < 128 - off, tiles[n], tiles[n + 1])
                wp[q * 4 + r, 0:224, n * 128 : (n + 1) * 128] = block.astype(BF16)
        return carry

    lax.fori_loop(0, 4, relay, 0)

    offset = (224 * (2 * yh + c)) % 128
    at, feature = iota((128, 256), 0), iota((128, 256), 1)
    head = 96 + ((feature + offset) >> 7)
    chosen = ((at == head) | (at == head + 16)) & (feature < 224)
    selector[...] = jnp.where(chosen, 1.0, 0.0).astype(BF16)

    mine = yl * 4 + 2 * yh + c

    def pass_on(p):
        @pl.when((p >= 4) & (p != 8) & (p <= 12))
        def _():
            arrived(ztile.at[p], r_rs.at[p])

        def forward(to_p, way):
            pltpu.make_async_remote_copy(
                src_ref=ztile.at[p], dst_ref=ztile.at[to_p], send_sem=f_ss, recv_sem=r_rs.at[to_p],
                device_id=dev(z_=(z + 16 + way) % 16), device_id_type=MESH,
            ).start()

        @pl.when((p >= 4) & (p <= 7))
        def _():
            forward(p - 4, 4)

        @pl.when((p >= 9) & (p <= 11))
        def _():
            forward(p + 4, -4)

    def slot_of(zs):
        return (zs - z + 24) % 16

    for zs in range(16):
        pass_on(slot_of(zs))
    for half in range(2):
        for zs in range(8 * half, 8 * half + 8):
            p = slot_of(zs)

            @pl.when((p < 4) | (p > 12))
            def _():
                arrived(ztile.at[p], r_rs.at[p])

        rows = pl.ds(64 * half, 64)
        for zs in range(8 * half, 8 * half + 8):
            xf[0, 8 * zs : 8 * zs + 8, :] = ztile[slot_of(zs)]
        packed = xf[0, rows, :].astype(BF16)
        qall[mine, rows, :] = packed
        qsend[rows, :] = packed
        for at, (dy, dc) in enumerate(partners):
            send(
                qsend.at[rows], qall.at[mine, rows], qa_ss.at[half, at], qa_rs.at[half, mine],
                dev(y_=(y + dy) % 4, c_=(c + dc) % 2),
            )

    def by_head(half):
        for dy, dc in partners:
            source = (y + dy) % 4
            source = (source % 2) * 4 + (source // 2) * 2 + (c + dc) % 2
            arrived(qall.at[source, pl.ds(64 * half, 64)], qa_rs.at[half, source])
        lane = iota((32, 128), 1)
        xf[:, 64 * half : 64 * half + 64, :] = qall[:, 64 * half : 64 * half + 64, :].astype(F32)
        for side in range(2):
            pieces = [xf[side * 4 + n // 2, pl.ds(64 * half + n % 2, 32, stride=2), :] for n in range(8)]
            starts = [224 * (n // 2) + 128 * (n % 2) for n in range(8)]
            sizes = [128 if n % 2 == 0 else 96 for n in range(8)]
            for h in range(7):
                head = None
                for n in range(8):
                    low = max(starts[n], 128 * h)
                    high = min(starts[n] + sizes[n], 128 * h + 128)
                    if low < high:
                        shift = (starts[n] - 128 * h) % 128
                        moved = pltpu.roll(pieces[n], shift, 1) if shift else pieces[n]
                        if head is None:
                            head = moved
                        else:
                            head = jnp.where(lane < low - 128 * h, head, moved)
                if h <= 3:
                    qf[half, side * 2, h * 32 : (h + 1) * 32, :] = head
                if h >= 3:
                    qf[half, side * 2 + 1, (h - 3) * 32 : (h - 2) * 32, :] = head

    def attend(half, chunks, old_top):
        rows = qf[half].reshape(512, 128).astype(BF16)
        top = None
        for n, k in enumerate(chunks):
            scores = lax.dot_general(rows, kbuf[k], ROW_DIMS, preferred_element_type=F32)
            s_ref[:, n * 512 : (n + 1) * 512] = scores
            for m in range(4):
                part = scores[:, m * 128 : (m + 1) * 128]
                top = part if top is None else jnp.maximum(top, part)
        top = (jnp.max(top, axis=1, keepdims=True) * SCALE).astype(BF16).astype(F32)
        top = jnp.broadcast_to(top, (512, 128))
        if old_top is not None:
            top = jnp.maximum(top, old_top)
        total, values = 0.0, 0.0
        for n, k in enumerate(chunks):
            probs = []
            for m in range(4):
                at = n * 512 + m * 128
                part = jnp.exp2(s_ref[:, at : at + 128] * SCALE - top)
                total = total + part
                probs.append(part.astype(BF16))
            probs = jnp.concatenate(probs, axis=1)
            values = values + jnp.dot(probs, vbuf[k], preferred_element_type=F32)
        return top, jnp.broadcast_to(jnp.sum(total, axis=1, keepdims=True), (512, 128)), values

    def keep(top, total, values):
        acc[...] = values.reshape(4, 128, 128)
        tops[...] = top.reshape(4, 128, 128)
        totals[...] = total.reshape(4, 128, 128)

    def to_owners(half):
        lane = iota((32, 128), 1)
        for n in range(4):
            to_y, to_yh = 2 * (n % 2) + n // 2, n % 2
            dy = (to_y - y + 4) % 4
            for to_c in range(2):
                start = 64 * to_yh + 224 * to_c
                off = start % 128
                js = [min(start // 128 + i, 3) for i in range(3)]
                picked = [[part[n, 32 * j : 32 * j + 32, :] for j in js] for part in (acc, tops, totals)]
                moved = [pltpu.roll(part, 128 - off, 1) if off else part for part in picked[0]]
                first = jnp.where(lane < 128 - off, moved[0], moved[1])
                osend[half, n, to_c, 0:32, :] = first.astype(BF16)
                second = jnp.where(lane < 128 - off, moved[1], moved[2])
                second = jnp.where(lane < 96, second, stats(picked[1], picked[2], True))
                osend[half, n, to_c, 32:64, :] = second.astype(BF16)
                here = (dy == 0) & (c == to_c)

                @pl.when(jnp.logical_not(here))
                def _():
                    pltpu.make_async_remote_copy(
                        src_ref=osend.at[half, n, to_c], dst_ref=orecv.at[half, dy * 2 + c], send_sem=o_ss.at[half],
                        recv_sem=o_rs.at[half, dy * 2 + c], device_id=dev(y_=to_y, c_=to_c), device_id_type=MESH,
                    ).start()

                @pl.when(here)
                def _():
                    orecv[half, c] = osend[half, n, to_c]

    lane = iota((1, 128), 1)
    is_top = (lane >= 96) & (lane < 99)
    own_tile = pl.ds(pl.multiple_of(8 * z, 8), 8)

    def merge_partners(half):
        for dy in (2, 1, 3):
            for from_c in range(2):
                arrived(orecv.at[half, dy * 2 + from_c], o_rs.at[half, dy * 2 + from_c])
        arrived(orecv.at[half, 1 - c], o_rs.at[half, 1 - c])
        firsts = [orecv[half, k, 0:32, :].astype(F32) for k in range(8)]
        seconds = [orecv[half, k, 32:64, :].astype(F32) for k in range(8)]
        top = seconds[0]
        for k in range(1, 8):
            top = jnp.maximum(top, seconds[k])
        weight = [jnp.where(is_top, jnp.exp2(part - top), 0.0) for part in seconds]
        wide = spread(jnp.concatenate(weight, axis=0), selector[...])
        first, second, total = 0.0, 0.0, 0.0
        for k in range(8):
            total = total + weight[k] * (pltpu.roll(seconds[k], 124, 1) + pltpu.roll(seconds[k], 120, 1))
            first = first + wide[0][32 * k : 32 * k + 32] * firsts[k]
            second = second + wide[1][32 * k : 32 * k + 32] * seconds[k]
        second = second + jnp.where(is_top, top, 0.0) + pltpu.roll(total, 4, 1)
        zsend[pl.ds(64 * half, 32, stride=2), :] = first
        zsend[pl.ds(64 * half + 1, 32, stride=2), :] = second
        for zs in range(8 * half, 8 * half + 8):

            @pl.when(z != zs)
            def _():
                pltpu.make_async_remote_copy(
                    src_ref=zsend.at[pl.ds(8 * zs, 8)], dst_ref=zrecv.at[own_tile], send_sem=z_ss, recv_sem=z_rs.at[z],
                    device_id=dev(z_=zs), device_id_type=MESH,
                ).start()

    by_head(0)
    local[0].wait()
    local[1].wait()
    for d in (1, 3):
        arrived(kbuf.at[d], k_rs.at[d])
        arrived(vbuf.at[d], v_rs.at[d])
    keep(*attend(0, (0, 1, 3), None))
    for copy in local[3:]:
        copy.wait()
    sfx[gx] = sbuf[x, 2 * yh + c]
    arrived(kbuf.at[2], k_rs.at[2])
    arrived(vbuf.at[2], v_rs.at[2])
    old_top = tops[...].reshape(512, 128)
    top, total, values = attend(0, (2,), old_top)
    scale = jnp.exp2(old_top - top)
    keep(
        top, total + scale * totals[...].reshape(512, 128), values + scale * acc[...].reshape(512, 128)
    )
    to_owners(0)

    for d in range(1, 16):
        to = (gx + d) % 16
        send(sbuf.at[to // 4, to % 4], sfx.at[gx], s_ss.at[d], s_rs.at[gx], (to, gy))

    by_head(1)
    keep(*attend(1, (0, 1, 2, 3), None))
    to_owners(1)

    merge_partners(0)

    for d in range(1, 16):
        source = (gx + d) % 16
        arrived(sfx.at[source], s_rs.at[source])
    mine = 2 * yh + c
    own = [qf[z // 8, yl * 2 + n, pl.ds((z % 8) * 4 + mine, 4, stride=32), :] for n in range(2)]
    own = jnp.concatenate(own, axis=0).astype(BF16)
    suffix_keys = sfx[:, 0].reshape(256, 128)
    suffix_values = sfx[:, 1].reshape(256, 128)
    scores = lax.dot_general(own, suffix_keys, ROW_DIMS, preferred_element_type=F32) * SCALE
    live = iota((8, 256), 1) < len_ref[mine]
    scores = jnp.where(live, scores, -1e30)
    top = jnp.max(scores, axis=1, keepdims=True)
    probs = jnp.where(live, jnp.exp2(scores - top), 0.0)
    total = jnp.sum(probs, axis=1, keepdims=True)
    values = jnp.dot(probs.astype(BF16), suffix_values, preferred_element_type=F32)
    for to in range(4):
        start = 64 * (to // 2) + 224 * (to % 2)
        off = start % 128
        picked = []
        for part in (values, top, total):
            rows = [4 * (to // 2) + min(start // 128 + i, 3) for i in range(3)]
            picked.append([part[row : row + 1] for row in rows])
        moved = [pltpu.roll(part, 128 - off, 1) if off else part for part in picked[0]]
        ssend[to, 0:1, :] = jnp.where(lane < 128 - off, moved[0], moved[1])
        second = jnp.where(lane < 128 - off, moved[1], moved[2])
        ssend[to, 1:2, :] = jnp.where(lane < 96, second, stats(picked[1], picked[2], False))
    near_by = ((1, 0), (1, 1), (0, 1))
    for at, (dyh, dc) in enumerate(near_by):
        to_yh, to_c = (yh + dyh) % 2, (c + dc) % 2
        to = dev(y_=(y + 2 * dyh) % 4, c_=to_c)
        send(ssend.at[2 * to_yh + to_c], srecv.at[mine], h_ss.at[at], h_rs.at[mine], to)
    srecv[mine] = ssend[mine]

    merge_partners(1)
    zrecv[own_tile, :] = zsend[own_tile, :]
    for dyh, dc in near_by:
        source = 2 * ((yh + dyh) % 2) + (c + dc) % 2
        arrived(srecv.at[source], h_rs.at[source])
    tail = iota((8, 128), 0) < 4
    zeros = jnp.zeros((4, 128), F32)
    suffix_first = jnp.concatenate([srecv[t, 0:1, :] for t in range(4)] + [zeros], axis=0)
    suffix_second = jnp.concatenate([srecv[t, 1:2, :] for t in range(4)] + [zeros], axis=0)
    suffix_second = jnp.where(tail | jnp.logical_not(is_top), suffix_second, -1e30)

    for copy in sent:
        copy.wait_send()
    sent.clear()
    pltpu.make_async_remote_copy(
        src_ref=ztile.at[pl.ds(0, 7)], dst_ref=ztile.at[pl.ds(0, 7)], send_sem=f_ss, recv_sem=r_rs.at[8],
        device_id=dev(c_=1 - c), device_id_type=MESH,
    ).wait_send()

    for half in range(2):
        pltpu.make_async_remote_copy(
            src_ref=orecv.at[half, pl.ds(0, 7)], dst_ref=orecv.at[half, pl.ds(0, 7)], send_sem=o_ss.at[half],
            recv_sem=o_rs.at[half, 0], device_id=dev(c_=1 - c), device_id_type=MESH,
        ).wait_send()

    for hops in range(1, 16):
        source = (z + hops) % 16
        arrived(zrecv.at[pl.ds(pl.multiple_of(8 * source, 8), 8)], z_rs.at[source])
    first = zrecv[pl.ds(0, 64, stride=2), :]
    second = zrecv[pl.ds(1, 64, stride=2), :]
    firsts = [first[8 * k : 8 * k + 8] for k in range(8)] + [suffix_first]
    seconds = [second[8 * k : 8 * k + 8] for k in range(8)] + [suffix_second]
    top = seconds[0]
    for k in range(1, 9):
        top = jnp.maximum(top, seconds[k])
    top = jnp.maximum(top, pltpu.roll(top, 4, 0))
    weight = [jnp.where(is_top, jnp.exp2(part - top), 0.0) for part in seconds]
    wide = spread(jnp.concatenate(weight, axis=0), selector[...])
    first, second, total = 0.0, 0.0, 0.0
    for k in range(9):
        first = first + wide[0][8 * k : 8 * k + 8] * firsts[k]
        second = second + wide[1][8 * k : 8 * k + 8] * seconds[k]
        total = total + weight[k] * pltpu.roll(seconds[k], 124, 1)
    first = first + pltpu.roll(first, 4, 0)
    second = second + pltpu.roll(second, 4, 0)
    total = total + pltpu.roll(total, 4, 0)
    wide = spread(total, selector[...])
    second = jnp.where(lane < 96, second / wide[1], 0.0)
    features = jnp.concatenate([first / wide[0], second], axis=1).astype(BF16)

    row = iota((8, 128), 0)
    others = [(dx, dyh, dc) for dx in range(4) for dyh in range(2) for dc in range(2)]
    others.sort(key=lambda move: -(min(move[0], 4 - move[0]) + 2 * move[1] + move[2]))
    for at, (dx, dyh, dc) in enumerate(others):
        to = ((x + dx) % 4) * 4 + ((yh + dyh) % 2) * 2 + (c + dc) % 2
        product = jnp.dot(features, wp[to], preferred_element_type=F32)
        tile = jnp.where(row < 4, product[:, 0:128], product[:, 128:256])
        if at < 15:
            psend[at] = tile
            send(psend.at[at], precv.at[at], p_ss.at[at], p_rs.at[at], (to, gy))
    for at in range(15):
        arrived(precv.at[at], p_rs.at[at])
    for at in range(15):
        tile = tile + precv[at]
    pltpu.make_async_remote_copy(
        src_ref=zsend.at[pl.ds(0, 120)], dst_ref=zsend.at[pl.ds(0, 120)], send_sem=z_ss, recv_sem=z_rs.at[0],
        device_id=dev(c_=1 - c), device_id_type=MESH,
    ).wait_send()
    result = tile
    o_ref[:, 0:128] = result[0:4].astype(BF16)
    o_ref[:, 128:224] = result[4:8, 0:96].astype(BF16)
    for copy in sent:
        copy.wait_send()


def on_device(query, keys, values, suffix_keys, suffix_values, lengths, out_weight):
    hbm = pl.BlockSpec(memory_space=pltpu.HBM)
    dma = pltpu.SemaphoreType.DMA
    return pl.pallas_call(
        kernel,
        out_shape=jax.ShapeDtypeStruct((4, 224), BF16),
        in_specs=[hbm] * 7,
        out_specs=pl.BlockSpec(memory_space=pltpu.VMEM),
        scratch_shapes=[
            pltpu.VMEM((4, 224), BF16),
            pltpu.SMEM((4,), jnp.int32),
            pltpu.VMEM((4, 512, 128), BF16),
            pltpu.VMEM((4, 512, 128), BF16),
            pltpu.VMEM((224, 3584), BF16),
            pltpu.VMEM((16, 256, 256), BF16),
            pltpu.VMEM((4, 4, 2, 16, 128), BF16),
            pltpu.VMEM((16, 2, 16, 128), BF16),
            pltpu.VMEM((16, 8, 128), F32),
            pltpu.VMEM((128, 128), BF16),
            pltpu.VMEM((8, 128, 128), BF16),
            pltpu.VMEM((8, 128, 128), F32),
            pltpu.VMEM((2, 4, 128, 128), F32),
            pltpu.VMEM((512, 2048), F32),
            pltpu.VMEM((4, 128, 128), F32),
            pltpu.VMEM((4, 128, 128), F32),
            pltpu.VMEM((4, 128, 128), F32),
            pltpu.VMEM((128, 256), BF16),
            pltpu.VMEM((2, 4, 2, 64, 128), BF16),
            pltpu.VMEM((2, 8, 64, 128), BF16),
            pltpu.VMEM((128, 128), F32),
            pltpu.VMEM((128, 128), F32),
            pltpu.VMEM((4, 8, 128), F32),
            pltpu.VMEM((4, 8, 128), F32),
            pltpu.VMEM((16, 8, 128), F32),
            pltpu.VMEM((16, 8, 128), F32),
            dma((13,)),
            dma((4,)), dma((4,)), dma((4,)), dma((4,)),
            dma((16,)), dma((16,)),
            dma((16,)), dma((16,)), dma,
            dma((2, 7)), dma((2, 8)),
            dma((2,)), dma((2, 8)),
            dma, dma((16,)),
            dma((3,)), dma((4,)),
            dma((16,)), dma((16,)),
        ],
        compiler_params=pltpu.CompilerParams(
            collective_id=0, has_side_effects=True, vmem_limit_bytes=56 * 2**20
        ),
        name="decode_attention",
    )(query, keys, values, suffix_keys, suffix_values, lengths, out_weight)


def solution(mesh):
    return jax.shard_map(
        on_device,
        mesh=mesh,
        in_specs=(
            P("gy", "gx"),
            P(("gx", "gy"), None),
            P(("gx", "gy"), None),
            P("gy", "gx", None),
            P("gy", "gx", None),
            P("gy"),
            P("gx", None),
        ),
        out_specs=P("gy", "gx"),
        check_vma=False,
    )
```

time: 56.1 us -> 52 us (0.927)
  Pallas kernels: 54.6 us -> 50.5 us
    pallas_call x1, Pallas kernels: 54.6 us -> 50.5 us  [on_device(): pl.pallas_call(kernel, out_shape=jax.ShapeDtypeStruct((4, 224), BF16), in...]
where the time goes in v3:
time: 52 us; the launch traced here: 51.7 us
  Pallas kernels  50.5 us (97%)
  local copies, waits for them, and re-layouts  1.26 us (2%)
    pallas_call x1, Pallas kernels, on_device(): pl.pallas_call(kernel, out_shape=jax.ShapeDtypeStruct((4, 224), BF16), in...  50.5 us
    unnamed x1, local copies, waits for them, and re-layouts  1.26 us

profile of v3, /device:TPU:1, one launch (start us, length us, event | category | flops | bytes accessed | tf_op | source)
XLA Modules:
  0.0 51.7 jit_solution(4039629083768327494)
XLA Ops:
  0.0 50.5 %decode_attention.1 = bf16[4,224]{1,0:T(4,128)(2,1)} custom-call(bf16[4,224]{1,0:T(4,128)(2,1)} %q_hbm.1, bf16[512,512]{1,0:T(8,128)(2,1)} %k_hbm.1, bf16[512,512]{1,0:T(8,128)(2,1)} %v_hbm.1, bf16[4,16,512]{2,1,0:T(8,128)(2,1)} %sk_hbm.1, bf16[4,16,512]{2,1,0:T(8,128)(2,1)} %sv_hbm.1, s32[4]{0:T(128)} %len_hbm.1, bf16[224,3584]{1,0:T(8,128)(2,1)} %w_hbm.1), custom_call_target="tpu_custom_call" | custom-call | tf_op jit(solution)/shard_map/decode_attention/pallas_call | solution.py:458
  50.5 1.3 %copy.9 = bf16[4,224]{1,0:T(4,128)(2,1)} copy(bf16[4,224]{1,0:T(4,128)(2,1)} %decode_attention.1) | data formatting | bytes 3584

commit v4 on v3

--- a/solution.py
+++ b/solution.py
@@ -314,16 +314,31 @@
                     device_id=dev(z_=zs), device_id_type=MESH,
                 ).start()
 
-    by_head(0)
     local[0].wait()
     local[1].wait()
+    for copy in local[3:]:
+        copy.wait()
     for d in (1, 3):
         arrived(kbuf.at[d], k_rs.at[d])
         arrived(vbuf.at[d], v_rs.at[d])
+
+    def send_suffix(dx, to_yh, to_c):
+        to_x, slot = (x + dx) % 4, dx * 4 + (yh + to_yh) % 2 * 2 + (c + to_c) % 2
+        to_yh, to_c = (yh + to_yh) % 2, (c + to_c) % 2
+        send(
+            sbuf.at[to_x, 2 * to_yh + to_c], sfx.at[gx], s_ss.at[slot], s_rs.at[gx],
+            (to_x * 4 + 2 * to_yh + to_c, gy),
+        )
+
+    sfx[gx] = sbuf[x, 2 * yh + c]
+    for dx in (1, 3, 0):
+        for to_yh in range(2):
+            for to_c in range(2):
+                if dx or to_yh or to_c:
+                    send_suffix(dx, to_yh, to_c)
+
+    by_head(0)
     keep(*attend(0, (0, 1, 3), None))
-    for copy in local[3:]:
-        copy.wait()
-    sfx[gx] = sbuf[x, 2 * yh + c]
     arrived(kbuf.at[2], k_rs.at[2])
     arrived(vbuf.at[2], v_rs.at[2])
     old_top = tops[...].reshape(512, 128)
@@ -334,9 +349,9 @@
     )
     to_owners(0)
 
-    for d in range(1, 16):
-        to = (gx + d) % 16
-        send(sbuf.at[to // 4, to % 4], sfx.at[gx], s_ss.at[d], s_rs.at[gx], (to, gy))
+    for to_yh in range(2):
+        for to_c in range(2):
+            send_suffix(2, to_yh, to_c)
 
     by_head(1)
     keep(*attend(1, (0, 1, 2, 3), None))

time: 52 us -> 51.2 us (0.985)
  Pallas kernels: 50.5 us -> 49.7 us
    pallas_call x1, Pallas kernels: 50.5 us -> 49.7 us  [on_device(): pl.pallas_call(kernel, out_shape=jax.ShapeDtypeStruct((4, 224), BF16), in...]
where the time goes in v4:
time: 51.2 us; the launch traced here: 51 us
  Pallas kernels  49.7 us (97%)
  local copies, waits for them, and re-layouts  1.26 us (2%)
    pallas_call x1, Pallas kernels, on_device(): pl.pallas_call(kernel, out_shape=jax.ShapeDtypeStruct((4, 224), BF16), in...  49.7 us
    unnamed x1, local copies, waits for them, and re-layouts  1.26 us

profile of v4, /device:TPU:1, one launch (start us, length us, event | category | flops | bytes accessed | tf_op | source)
XLA Modules:
  0.0 51.0 jit_solution(3578856277707991132)
XLA Ops:
  0.0 49.7 %decode_attention.1 = bf16[4,224]{1,0:T(4,128)(2,1)} custom-call(bf16[4,224]{1,0:T(4,128)(2,1)} %q_hbm.1, bf16[512,512]{1,0:T(8,128)(2,1)} %k_hbm.1, bf16[512,512]{1,0:T(8,128)(2,1)} %v_hbm.1, bf16[4,16,512]{2,1,0:T(8,128)(2,1)} %sk_hbm.1, bf16[4,16,512]{2,1,0:T(8,128)(2,1)} %sv_hbm.1, s32[4]{0:T(128)} %len_hbm.1, bf16[224,3584]{1,0:T(8,128)(2,1)} %w_hbm.1), custom_call_target="tpu_custom_call" | custom-call | tf_op jit(solution)/shard_map/decode_attention/pallas_call | solution.py:473
  49.7 1.3 %copy.9 = bf16[4,224]{1,0:T(4,128)(2,1)} copy(bf16[4,224]{1,0:T(4,128)(2,1)} %decode_attention.1) | data formatting | bytes 3584

commit v5 on v4

--- a/solution.py
+++ b/solution.py
@@ -223,7 +223,7 @@
                     qf[half, side * 2 + 1, (h - 3) * 32 : (h - 2) * 32, :] = head
 
     def attend(half, chunks, old_top):
-        rows = qf[half].reshape(512, 128).astype(BF16)
+        rows = qf[half, 0:4].reshape(512, 128).astype(BF16)
         top = None
         for n, k in enumerate(chunks):
             scores = lax.dot_general(rows, kbuf[k], ROW_DIMS, preferred_element_type=F32)
@@ -488,7 +488,7 @@
             pltpu.VMEM((128, 128), BF16),
             pltpu.VMEM((8, 128, 128), BF16),
             pltpu.VMEM((8, 128, 128), F32),
-            pltpu.VMEM((2, 4, 128, 128), F32),
+            pltpu.VMEM((2, 6, 128, 128), F32),
             pltpu.VMEM((512, 2048), F32),
             pltpu.VMEM((4, 128, 128), F32),
             pltpu.VMEM((4, 128, 128), F32),
@@ -496,8 +496,8 @@
             pltpu.VMEM((128, 256), BF16),
             pltpu.VMEM((2, 4, 2, 64, 128), BF16),
             pltpu.VMEM((2, 8, 64, 128), BF16),
-            pltpu.VMEM((128, 128), F32),
-            pltpu.VMEM((128, 128), F32),
+            pltpu.VMEM((144, 128), F32),
+            pltpu.VMEM((144, 128), F32),
             pltpu.VMEM((4, 8, 128), F32),
             pltpu.VMEM((4, 8, 128), F32),
             pltpu.VMEM((16, 8, 128), F32),

time: 51.2 us -> 51.2 us (level)
  no operation moved by 1% of the time
where the time goes in v5:
time: 51.2 us; the launch traced here: 51 us
  Pallas kernels  49.7 us (97%)
  local copies, waits for them, and re-layouts  1.26 us (2%)
    pallas_call x1, Pallas kernels, on_device(): pl.pallas_call(kernel, out_shape=jax.ShapeDtypeStruct((4, 224), BF16), in...  49.7 us
    unnamed x1, local copies, waits for them, and re-layouts  1.26 us

profile of v5, /device:TPU:1, one launch (start us, length us, event | category | flops | bytes accessed | tf_op | source)
XLA Modules:
  0.0 51.0 jit_solution(7071773761778852482)
XLA Ops:
  0.0 49.7 %decode_attention.1 = bf16[4,224]{1,0:T(4,128)(2,1)} custom-call(bf16[4,224]{1,0:T(4,128)(2,1)} %q_hbm.1, bf16[512,512]{1,0:T(8,128)(2,1)} %k_hbm.1, bf16[512,512]{1,0:T(8,128)(2,1)} %v_hbm.1, bf16[4,16,512]{2,1,0:T(8,128)(2,1)} %sk_hbm.1, bf16[4,16,512]{2,1,0:T(8,128)(2,1)} %sv_hbm.1, s32[4]{0:T(128)} %len_hbm.1, bf16[224,3584]{1,0:T(8,128)(2,1)} %w_hbm.1), custom_call_target="tpu_custom_call" | custom-call | tf_op jit(solution)/shard_map/decode_attention/pallas_call | solution.py:473
  49.7 1.3 %copy.9 = bf16[4,224]{1,0:T(4,128)(2,1)} copy(bf16[4,224]{1,0:T(4,128)(2,1)} %decode_attention.1) | data formatting | bytes 3584
